TPU v7x, 1024 devices: a whole 4x8x16 slice. The times are simulated.
1024 devices in a mesh: ctx: 256 (over x, y_hi, z), head: 4 (over y_lo, core).
Axes of the slice: x: 4, y: 8 (y_hi: 4, y_lo: 2; y = y_hi * 2 + y_lo), z: 16, core: 2. Of those that a mesh axis runs over, the one named last changes fastest.
Arguments:
- queries: bfloat16 [32768, 8, 4, 128], P('ctx', 'head'), may hold values from -8 to 8
- keys: bfloat16 [32768, 4, 128], P('ctx'), may hold values from -8 to 8
- values: bfloat16 [32768, 4, 128], P('ctx'), may hold values from -6 to 6
- out_grad: bfloat16 [32768, 8, 4, 128], P('ctx', 'head'), may hold values from -6 to 6
- lengths: int32 [128], replicated, may hold values from 1 to 384, as said below
Outputs:
- query_grad: bfloat16 [32768, 8, 4, 128], P('ctx', 'head')
- key_grad: bfloat16 [32768, 4, 128], P('ctx', 'head')
- value_grad: bfloat16 [32768, 4, 128], P('ctx', 'head')
Inputs may be any that keep to these rules, and one draw needn't show every extreme that they name: The 128 lengths sum to 32768; the first document is the longest, exactly 384 tokens.
All inputs are finite; a program needn't handle non-finite values.
Results may differ from a plain program's by a relative error of at most 0.008.
Values may be sent and summed in bfloat16 or wider, within the bound.
A program may use at most 32 MiB of HBM per device.

v0:
```python
from functools import partial

import jax
import jax.numpy as jnp
from jax import lax
from jax.sharding import PartitionSpec as P

SPAN = 4


lowest = -1e30


def passed_along(x, axis, by):
    size = lax.axis_size(axis)
    pairs = [(i, i + by) for i in range(size) if 0 <= i + by < size]
    return lax.ppermute(x, axis, pairs)


def from_behind(value, axis, steps):
    count = lax.axis_size(axis)
    pairs = [(source, (source + steps) % count) for source in range(count)]
    return lax.ppermute(value, axis, pairs)


def block_docs(ends, anchor, width):
    position = anchor * width + jnp.arange(width, dtype=jnp.int32)
    document = jnp.sum((ends[None, :] <= position[:, None]).astype(jnp.int32), axis=1)
    return (position, document)


def run_tile(compute):
    result = compute()
    return result


def attend_back(queries, keys, values, out_grad, lengths):
    width = keys.shape[0]
    factor = keys.shape[2] ** (-0.5)
    cycle_size = lax.axis_size("ctx")
    own_index = lax.axis_index("ctx")
    ends = jnp.cumsum(lengths)
    own_pos, own_doc = block_docs(ends, own_index, width)

    def visible(shift_count):
        anchor = (own_index - shift_count) % cycle_size
        key_pos, key_doc = block_docs(ends, anchor, width)
        return (key_pos[None, :] <= own_pos[:, None]) & (key_doc[None, :] == own_doc[:, None])

    def scores(key_block):
        return (
            jnp.einsum("pjgd,tgd->pjgt", queries, key_block, preferred_element_type=jnp.float32)
            * factor
        )

    def products(value_block):
        return jnp.einsum(
            "pjgd,tgd->pjgt", out_grad, value_block, preferred_element_type=jnp.float32
        )

    def stats_update(carry, key_block, value_block, allowed):
        peak, total, weighted = carry
        wide_mask = allowed[:, None, None, :]
        score = scores(key_block)
        dprob = products(value_block)
        new_peak = jnp.maximum(peak, jnp.max(jnp.where(wide_mask, score, lowest), axis=-1))
        expo = jnp.where(wide_mask, jnp.exp(score - new_peak[..., None]), 0.0)
        rescale = jnp.exp(peak - new_peak)
        return (
            new_peak,
            total * rescale + jnp.sum(expo, axis=-1),
            weighted * rescale + jnp.sum(expo * dprob, axis=-1),
        )

    stat_shape = queries.shape[:3]
    carry = (
        jnp.full(stat_shape, lowest, jnp.float32),
        jnp.zeros(stat_shape, jnp.float32),
        jnp.zeros(stat_shape, jnp.float32),
    )
    visitor = (keys, values)
    kept = []
    for shift_count in range(SPAN):
        allowed = visible(shift_count)
        carry = run_tile(partial(stats_update, carry, visitor[0], visitor[1], allowed))
        kept.append(visitor)
        if shift_count + 1 < SPAN:
            visitor = passed_along((visitor[0], visitor[1]), "ctx", 1)
    peak, total, weighted = carry
    delta = weighted / total
    pair_shape = (width, keys.shape[1], 2, keys.shape[2])

    def grads_tile(key_block, value_block, allowed):
        wide_mask = allowed[:, None, None, :]
        score = scores(key_block)
        prob = jnp.where(wide_mask, jnp.exp(score - peak[..., None]) / total[..., None], 0.0)
        dprob = products(value_block)
        dscore = (prob * (dprob - delta[..., None])).astype(jnp.bfloat16)
        prob_low = prob.astype(jnp.bfloat16)
        query_part = jnp.einsum(
            "pjgt,tgd->pjgd", dscore, key_block, preferred_element_type=jnp.float32
        )
        key_part = (
            jnp.einsum("pjgt,pjgd->tgd", dscore, queries, preferred_element_type=jnp.float32)
            * factor
        )
        value_part = jnp.einsum(
            "pjgt,pjgd->tgd", prob_low, out_grad, preferred_element_type=jnp.float32
        )
        return (query_part, jnp.stack([key_part, value_part], axis=2))

    query_acc = jnp.zeros(queries.shape, jnp.float32)
    visitor = (keys, values)
    carried = jnp.zeros(pair_shape, jnp.float32)
    for shift_count in range(SPAN):
        allowed = visible(shift_count)
        query_part, pair_part = run_tile(partial(grads_tile, visitor[0], visitor[1], allowed))
        query_acc = query_acc + query_part
        carried = carried + pair_part
        if shift_count + 1 < SPAN:
            visitor = passed_along((visitor[0], visitor[1]), "ctx", 1)
            carried = from_behind(carried, "ctx", 1)
    returned = from_behind(carried, "ctx", 1 - SPAN)
    query_grad = (query_acc * factor).astype(jnp.bfloat16)
    return (query_grad, returned)


def on_device(queries, keys, values, out_grad, lengths):
    query_grad, returned = attend_back(queries, keys, values, out_grad, lengths)
    summed = lax.psum_scatter(returned, "head", scatter_dimension=1, tiled=True)
    return (
        query_grad,
        summed[:, :, 0, :].astype(jnp.bfloat16),
        summed[:, :, 1, :].astype(jnp.bfloat16),
    )


def solution(mesh):
    in_specs = (
        P("ctx", "head", None, None),
        P("ctx", None, None),
        P("ctx", None, None),
        P("ctx", "head", None, None),
        P(),
    )
    out_specs = (P("ctx", "head", None, None), P("ctx", "head", None), P("ctx", "head", None))
    return jax.shard_map(
        on_device, mesh=mesh, in_specs=in_specs, out_specs=out_specs, check_vma=False
    )
```

profile of v0, /device:TPU:6, one launch (start us, length us, event | category | flops | bytes accessed | tf_op | source)
XLA Modules:
  0.0 183.0 jit_solution(1920445945917530650)
XLA Ops:
  0.6 0.0 copy-start
  0.7 1.0 copy.65
  1.6 4.3 %collective-permute-start = (bf16[128,4,128]{2,0,1:T(8,128)(2,1)S(1)}, bf16[128,4,128]{2,0,1:T(8,128)(2,1)S(1)}, u32[]{:S(2)}, u32[]{:S(2)}) collective-permute-start(bf16[128,4,128]{2,0,1:T(8,128)(2,1)S(1)} %copy.65), channel_id=1, source_target_pairs={{0,4},{4,8},{8,12},{12,16},{16,20},{20,24},{24,28},{28,32},{32,36}... | collective-permute-start | bytes 393224 | tf_op jit(solution)/shard_map/ppermute | solution.py:17
  5.9 0.0 copy-start.12
  6.0 0.0 copy-start.1
  6.0 4.4 %collective-permute-start.3 = (bf16[128,4,128]{2,0,1:T(8,128)(2,1)S(1)}, bf16[128,4,128]{2,0,1:T(8,128)(2,1)S(1)}, u32[]{:S(2)}, u32[]{:S(2)}) collective-permute-start(bf16[128,4,128]{2,0,1:T(8,128)(2,1)S(1)} %copy.71), channel_id=1, source_target_pairs={{0,4},{4,8},{8,12},{12,16},{16,20},{20,24},{24,28},{28,32},{32,36}... | collective-permute-start | bytes 393224 | tf_op jit(solution)/shard_map/ppermute | solution.py:17
  10.5 0.1 copy.62
  10.6 0.2 reduce-window.8
  10.8 0.1 reduce
  10.9 0.1 convert_reduce_fusion
  11.1 0.2 compare_and_fusion.3
  11.3 0.0 copy-start.6
  11.3 0.2 copy-done.3
  11.5 0.2 select_reduce_fusion.3
  11.8 20.0 %collective-permute-done = bf16[128,4,128]{2,0,1:T(8,128)(2,1)S(1)} collective-permute-done((bf16[128,4,128]{2,0,1:T(8,128)(2,1)S(1)}, bf16[128,4,128]{2,0,1:T(8,128)(2,1)S(1)}, u32[]{:S(2)}, u32[]{:S(2)}) %collective-permute-start) | collective-permute-done | bytes 131104 | tf_op jit(solution)/shard_map/ppermute | solution.py:17
  31.8 1.9 %collective-permute-start.1 = (bf16[128,4,128]{2,0,1:T(8,128)(2,1)S(1)}, bf16[128,4,128]{2,0,1:T(8,128)(2,1)S(1)}, u32[]{:S(2)}, u32[]{:S(2)}) collective-permute-start(bf16[128,4,128]{2,0,1:T(8,128)(2,1)S(1)} %collective-permute-done), channel_id=1, source_target_pairs={{0,4},{4,8},{8,12},{12,16},{16,20},{20,24},{24,28},{28,32},{32,36}... | collective-permute-start | bytes 393224 | tf_op jit(solution)/shard_map/ppermute | solution.py:17
  33.7 1.4 collective-permute-done.3
  35.0 1.9 %collective-permute-start.4 = (bf16[128,4,128]{2,0,1:T(8,128)(2,1)S(1)}, bf16[128,4,128]{2,0,1:T(8,128)(2,1)S(1)}, u32[]{:S(2)}, u32[]{:S(2)}) collective-permute-start(bf16[128,4,128]{2,0,1:T(8,128)(2,1)S(1)} %collective-permute-done.3), channel_id=1, source_target_pairs={{0,4},{4,8},{8,12},{12,16},{16,20},{20,24},{24,28},{28,32},{32,36}... | collective-permute-start | bytes 393224 | tf_op jit(solution)/shard_map/ppermute | solution.py:17
  36.9 0.2 select_reduce_fusion.2
  37.2 7.9 %collective-permute-done.1 = bf16[128,4,128]{2,0,1:T(8,128)(2,1)S(1)} collective-permute-done((bf16[128,4,128]{2,0,1:T(8,128)(2,1)S(1)}, bf16[128,4,128]{2,0,1:T(8,128)(2,1)S(1)}, u32[]{:S(2)}, u32[]{:S(2)}) %collective-permute-start.1) | collective-permute-done | bytes 131104 | tf_op jit(solution)/shard_map/ppermute | solution.py:17
  45.1 1.9 %collective-permute-start.2 = (bf16[128,4,128]{2,0,1:T(8,128)(2,1)S(1)}, bf16[128,4,128]{2,0,1:T(8,128)(2,1)S(1)}, u32[]{:S(2)}, u32[]{:S(2)}) collective-permute-start(bf16[128,4,128]{2,0,1:T(8,128)(2,1)S(1)} %collective-permute-done.1), channel_id=1, source_target_pairs={{0,4},{4,8},{8,12},{12,16},{16,20},{20,24},{24,28},{28,32},{32,36}... | collective-permute-start | bytes 393224 | tf_op jit(solution)/shard_map/ppermute | solution.py:17
  47.0 2.8 %collective-permute-done.4 = bf16[128,4,128]{2,0,1:T(8,128)(2,1)S(1)} collective-permute-done((bf16[128,4,128]{2,0,1:T(8,128)(2,1)S(1)}, bf16[128,4,128]{2,0,1:T(8,128)(2,1)S(1)}, u32[]{:S(2)}, u32[]{:S(2)}) %collective-permute-start.4) | collective-permute-done | bytes 131104 | tf_op jit(solution)/shard_map/ppermute | solution.py:17
  49.8 1.9 %collective-permute-start.5 = (bf16[128,4,128]{2,0,1:T(8,128)(2,1)S(1)}, bf16[128,4,128]{2,0,1:T(8,128)(2,1)S(1)}, u32[]{:S(2)}, u32[]{:S(2)}) collective-permute-start(bf16[128,4,128]{2,0,1:T(8,128)(2,1)S(1)} %collective-permute-done.4), channel_id=1, source_target_pairs={{0,4},{4,8},{8,12},{12,16},{16,20},{20,24},{24,28},{28,32},{32,36}... | collective-permute-start | bytes 393224 | tf_op jit(solution)/shard_map/ppermute | solution.py:17
  51.7 0.2 select_reduce_fusion.1
  52.0 6.8 %collective-permute-done.2 = bf16[128,4,128]{2,0,1:T(8,128)(2,1)S(1)} collective-permute-done((bf16[128,4,128]{2,0,1:T(8,128)(2,1)S(1)}, bf16[128,4,128]{2,0,1:T(8,128)(2,1)S(1)}, u32[]{:S(2)}, u32[]{:S(2)}) %collective-permute-start.2) | collective-permute-done | bytes 131104 | tf_op jit(solution)/shard_map/ppermute | solution.py:17
  58.8 0.2 select_reduce_fusion
  59.1 0.3 fusion.15
  59.3 0.2 fusion.17
  59.6 0.3 fusion.16
  59.8 3.4 %collective-permute-done.5 = bf16[128,4,128]{2,0,1:T(8,128)(2,1)S(1)} collective-permute-done((bf16[128,4,128]{2,0,1:T(8,128)(2,1)S(1)}, bf16[128,4,128]{2,0,1:T(8,128)(2,1)S(1)}, u32[]{:S(2)}, u32[]{:S(2)}) %collective-permute-start.5) | collective-permute-done | bytes 131104 | tf_op jit(solution)/shard_map/ppermute | solution.py:17
  63.2 0.3 select_reduce_fusion.4
  63.5 0.0 copy-start.10
  63.6 0.2 convolution_bitcast_fusion.10
  63.8 0.7 multiply_convert_fusion
  64.5 0.2 fusion.8
  64.7 0.1 pad_maximum_fusion
  64.8 1.9 %collective-permute-start.6 = (f32[128,4,2,128]{3,0,1,2:T(8,128)S(1)}, f32[128,4,2,128]{3,0,1,2:T(8,128)S(1)}, u32[]{:S(2)}, u32[]{:S(2)}) collective-permute-start(f32[128,4,2,128]{3,0,1,2:T(8,128)S(1)} %pad_maximum_fusion), channel_id=1, source_target_pairs={{0,4},{4,8},{8,12},{12,16},{16,20},{20,24},{24,28},{28,32},{32,36}... | collective-permute-start | bytes 1572872 | tf_op jit(solution)/shard_map/ppermute | solution.py:23
  66.7 0.2 fusion.10
  66.9 0.2 convolution_bitcast_fusion.8
  67.2 27.1 %collective-permute-done.6 = f32[128,4,2,128]{3,0,1,2:T(8,128)S(1)} collective-permute-done((f32[128,4,2,128]{3,0,1,2:T(8,128)S(1)}, f32[128,4,2,128]{3,0,1,2:T(8,128)S(1)}, u32[]{:S(2)}, u32[]{:S(2)}) %collective-permute-start.6) | collective-permute-done | bytes 524320 | tf_op jit(solution)/shard_map/ppermute | solution.py:23
  94.2 0.1 maximum_add_fusion
  94.3 1.9 %collective-permute-start.7 = (f32[128,4,2,128]{3,0,1,2:T(8,128)S(1)}, f32[128,4,2,128]{3,0,1,2:T(8,128)}, u32[]{:S(2)}, u32[]{:S(2)}) collective-permute-start(f32[128,4,2,128]{3,0,1,2:T(8,128)S(1)} %maximum_add_fusion), channel_id=1, source_target_pairs={{0,4},{4,8},{8,12},{12,16},{16,20},{20,24},{24,28},{28,32},{32,36}... | collective-permute-start | bytes 1572872 | tf_op jit(solution)/shard_map/ppermute | solution.py:23
  96.2 1.3 dynamic-slice
  97.5 0.2 fusion.12
  97.7 0.5 copy-done.7
  98.2 0.2 convolution_bitcast_fusion.6
  98.5 23.8 %collective-permute-done.7 = f32[128,4,2,128]{3,0,1,2:T(8,128)} collective-permute-done((f32[128,4,2,128]{3,0,1,2:T(8,128)S(1)}, f32[128,4,2,128]{3,0,1,2:T(8,128)}, u32[]{:S(2)}, u32[]{:S(2)}) %collective-permute-start.7) | collective-permute-done | bytes 524320 | tf_op jit(solution)/shard_map/ppermute | solution.py:23
  122.3 1.1 maximum_add_fusion.1
  123.4 1.9 %collective-permute-start.8 = (f32[128,4,2,128]{3,0,1,2:T(8,128)S(1)}, f32[128,4,2,128]{3,0,1,2:T(8,128)S(1)}, u32[]{:S(2)}, u32[]{:S(2)}) collective-permute-start(f32[128,4,2,128]{3,0,1,2:T(8,128)S(1)} %maximum_add_fusion.1), channel_id=1, source_target_pairs={{0,4},{4,8},{8,12},{12,16},{16,20},{20,24},{24,28},{28,32},{32,36}... | collective-permute-start | bytes 1572872 | tf_op jit(solution)/shard_map/ppermute | solution.py:23
  125.3 0.2 fusion.14
  125.5 0.3 fusion.32
  125.8 0.2 convolution_bitcast_fusion.4
  126.1 15.9 %collective-permute-done.8 = f32[128,4,2,128]{3,0,1,2:T(8,128)S(1)} collective-permute-done((f32[128,4,2,128]{3,0,1,2:T(8,128)S(1)}, f32[128,4,2,128]{3,0,1,2:T(8,128)S(1)}, u32[]{:S(2)}, u32[]{:S(2)}) %collective-permute-start.8) | collective-permute-done | bytes 524320 | tf_op jit(solution)/shard_map/ppermute | solution.py:23
  141.9 0.1 maximum_add_fusion.2
  142.0 0.0 copy-start.5
  142.0 2.1 %collective-permute-start.9 = (f32[128,4,2,128]{3,0,1,2:T(8,128)S(1)}, f32[128,4,2,128]{3,0,1,2:T(8,128)S(1)}, u32[]{:S(2)}, u32[]{:S(2)}) collective-permute-start(f32[128,4,2,128]{3,0,1,2:T(8,128)S(1)} %maximum_add_fusion.2), channel_id=1, source_target_pairs={{0,1012},{4,1016},{8,1020},{12,0},{16,4},{20,8},{24,12},{28,16},{3... | collective-permute-start | bytes 1572872 | tf_op jit(solution)/shard_map/ppermute | solution.py:23
  144.1 0.3 convolution_add_fusion.2
  144.4 0.3 convolution_add_fusion.1
  144.7 0.3 fusion.6
  145.0 0.9 copy.88
  145.9 19.7 %collective-permute-done.9 = f32[128,4,2,128]{3,0,1,2:T(8,128)S(1)} collective-permute-done((f32[128,4,2,128]{3,0,1,2:T(8,128)S(1)}, f32[128,4,2,128]{3,0,1,2:T(8,128)S(1)}, u32[]{:S(2)}, u32[]{:S(2)}) %collective-permute-start.9) | collective-permute-done | bytes 524320 | tf_op jit(solution)/shard_map/ppermute | solution.py:23
  165.5 16.2 %all-reduce.2 = bf16[128,4,2,128]{3,0,1,2:T(8,128)(2,1)S(1)} all-reduce(f32[128,4,2,128]{3,0,1,2:T(8,128)S(1)} %collective-permute-done.9), channel_id=2, replica_groups=mesh['ctx'=256,'head'=4] {'head'}, use_global_device_ids=true, to_apply=%region_18.19.clone | all-reduce | flops 131072 | bytes 786432
  181.8 0.6 dynamic-slice_convert_fusion
  182.4 0.6 slice_bitcast_fusion
  (24 shorter events, 0.1 us)
Async XLA Ops:
  0.6 58.4 %copy-start = (bf16[128,2,4,128]{3,2,1,0:T(4,128)(2,1)S(1)}, bf16[128,2,4,128]{3,2,1,0:T(4,128)(2,1)}, u32[]{:S(2)}) copy-start(bf16[128,2,4,128]{3,2,1,0:T(4,128)(2,1)} %param.8) | copy-start | bytes 786436
  0.6 5.3 %copy-start.2 = (bf16[128,4,128]{2,1,0:T(4,128)(2,1)S(1)}, bf16[128,4,128]{2,1,0:T(4,128)(2,1)}, u32[]{:S(2)}) copy-start(bf16[128,4,128]{2,1,0:T(4,128)(2,1)} %param.7) | copy-start | bytes 393220
  1.6 30.1 %collective-permute-start = (bf16[128,4,128]{2,0,1:T(8,128)(2,1)S(1)}, bf16[128,4,128]{2,0,1:T(8,128)(2,1)S(1)}, u32[]{:S(2)}, u32[]{:S(2)}) collective-permute-start(bf16[128,4,128]{2,0,1:T(8,128)(2,1)S(1)} %copy.65), channel_id=1, source_target_pairs={{0,4},{4,8},{8,12},{12,16},{16,20},{20,24},{24,28},{28,32},{32,36}... | collective-permute-start | bytes 393224 | tf_op jit(solution)/shard_map/ppermute | solution.py:17
  5.9 4.5 %copy-start.12 = (s32[128]{0:T(128)S(1)}, s32[128]{0:T(128)}, u32[]{:S(2)}) copy-start(s32[128]{0:T(128)} %param.9) | copy-start | bytes 1540
  6.0 5.3 %copy-start.1 = (bf16[128,2,4,128]{3,2,1,0:T(4,128)(2,1)S(1)}, bf16[128,2,4,128]{3,2,1,0:T(4,128)(2,1)}, u32[]{:S(2)}) copy-start(bf16[128,2,4,128]{3,2,1,0:T(4,128)(2,1)} %param.5) | copy-start | bytes 786436
  6.0 29.0 %collective-permute-start.3 = (bf16[128,4,128]{2,0,1:T(8,128)(2,1)S(1)}, bf16[128,4,128]{2,0,1:T(8,128)(2,1)S(1)}, u32[]{:S(2)}, u32[]{:S(2)}) collective-permute-start(bf16[128,4,128]{2,0,1:T(8,128)(2,1)S(1)} %copy.71), channel_id=1, source_target_pairs={{0,4},{4,8},{8,12},{12,16},{16,20},{20,24},{24,28},{28,32},{32,36}... | collective-permute-start | bytes 393224 | tf_op jit(solution)/shard_map/ppermute | solution.py:17
  10.6 0.9 copy-start.3
  11.3 52.5 %copy-start.6 = (pred[128,128]{0,1:T(8,128)(4,1)}, pred[128,128]{0,1:T(8,128)(4,1)S(1)}, u32[]{:S(2)}) copy-start(pred[128,128]{0,1:T(8,128)(4,1)S(1)} %get-tuple-element.39) | copy-start | bytes 49156
  31.8 13.4 %collective-permute-start.1 = (bf16[128,4,128]{2,0,1:T(8,128)(2,1)S(1)}, bf16[128,4,128]{2,0,1:T(8,128)(2,1)S(1)}, u32[]{:S(2)}, u32[]{:S(2)}) collective-permute-start(bf16[128,4,128]{2,0,1:T(8,128)(2,1)S(1)} %collective-permute-done), channel_id=1, source_target_pairs={{0,4},{4,8},{8,12},{12,16},{16,20},{20,24},{24,28},{28,32},{32,36}... | collective-permute-start | bytes 393224 | tf_op jit(solution)/shard_map/ppermute | solution.py:17
  35.0 14.8 %collective-permute-start.4 = (bf16[128,4,128]{2,0,1:T(8,128)(2,1)S(1)}, bf16[128,4,128]{2,0,1:T(8,128)(2,1)S(1)}, u32[]{:S(2)}, u32[]{:S(2)}) collective-permute-start(bf16[128,4,128]{2,0,1:T(8,128)(2,1)S(1)} %collective-permute-done.3), channel_id=1, source_target_pairs={{0,4},{4,8},{8,12},{12,16},{16,20},{20,24},{24,28},{28,32},{32,36}... | collective-permute-start | bytes 393224 | tf_op jit(solution)/shard_map/ppermute | solution.py:17
  45.1 6.9 %copy-start.4 = (bf16[128,4,128]{2,0,1:T(8,128)(2,1)}, bf16[128,4,128]{2,0,1:T(8,128)(2,1)S(1)}, u32[]{:S(2)}) copy-start(bf16[128,4,128]{2,0,1:T(8,128)(2,1)S(1)} %collective-permute-done.1) | copy-start | bytes 393220
  45.1 13.7 %collective-permute-start.2 = (bf16[128,4,128]{2,0,1:T(8,128)(2,1)S(1)}, bf16[128,4,128]{2,0,1:T(8,128)(2,1)S(1)}, u32[]{:S(2)}, u32[]{:S(2)}) collective-permute-start(bf16[128,4,128]{2,0,1:T(8,128)(2,1)S(1)} %collective-permute-done.1), channel_id=1, source_target_pairs={{0,4},{4,8},{8,12},{12,16},{16,20},{20,24},{24,28},{28,32},{32,36}... | collective-permute-start | bytes 393224 | tf_op jit(solution)/shard_map/ppermute | solution.py:17
  49.8 13.4 %collective-permute-start.5 = (bf16[128,4,128]{2,0,1:T(8,128)(2,1)S(1)}, bf16[128,4,128]{2,0,1:T(8,128)(2,1)S(1)}, u32[]{:S(2)}, u32[]{:S(2)}) collective-permute-start(bf16[128,4,128]{2,0,1:T(8,128)(2,1)S(1)} %collective-permute-done.4), channel_id=1, source_target_pairs={{0,4},{4,8},{8,12},{12,16},{16,20},{20,24},{24,28},{28,32},{32,36}... | collective-permute-start | bytes 393224 | tf_op jit(solution)/shard_map/ppermute | solution.py:17
  59.0 7.9 %copy-start.8 = (f32[128,2,4]{0,1,2:T(2,128)}, f32[128,2,4]{0,1,2:T(2,128)S(1)}, u32[]{:S(2)}) copy-start(f32[128,2,4]{0,1,2:T(2,128)S(1)} %get-tuple-element.25) | copy-start | bytes 12292
  63.5 3.4 %copy-start.10 = (f32[128,2,4]{0,1,2:T(2,128)}, f32[128,2,4]{0,1,2:T(2,128)S(1)}, u32[]{:S(2)}) copy-start(f32[128,2,4]{0,1,2:T(2,128)S(1)} %get-tuple-element.30) | copy-start | bytes 12292
  64.8 29.5 %collective-permute-start.6 = (f32[128,4,2,128]{3,0,1,2:T(8,128)S(1)}, f32[128,4,2,128]{3,0,1,2:T(8,128)S(1)}, u32[]{:S(2)}, u32[]{:S(2)}) collective-permute-start(f32[128,4,2,128]{3,0,1,2:T(8,128)S(1)} %pad_maximum_fusion), channel_id=1, source_target_pairs={{0,4},{4,8},{8,12},{12,16},{16,20},{20,24},{24,28},{28,32},{32,36}... | collective-permute-start | bytes 1572872 | tf_op jit(solution)/shard_map/ppermute | solution.py:23
  94.3 28.0 %collective-permute-start.7 = (f32[128,4,2,128]{3,0,1,2:T(8,128)S(1)}, f32[128,4,2,128]{3,0,1,2:T(8,128)}, u32[]{:S(2)}, u32[]{:S(2)}) collective-permute-start(f32[128,4,2,128]{3,0,1,2:T(8,128)S(1)} %maximum_add_fusion), channel_id=1, source_target_pairs={{0,4},{4,8},{8,12},{12,16},{16,20},{20,24},{24,28},{28,32},{32,36}... | collective-permute-start | bytes 1572872 | tf_op jit(solution)/shard_map/ppermute | solution.py:23
  97.5 0.7 copy-start.7
  97.5 0.7 copy-start.9
  97.5 0.7 copy-start.11
  123.4 18.6 %collective-permute-start.8 = (f32[128,4,2,128]{3,0,1,2:T(8,128)S(1)}, f32[128,4,2,128]{3,0,1,2:T(8,128)S(1)}, u32[]{:S(2)}, u32[]{:S(2)}) collective-permute-start(f32[128,4,2,128]{3,0,1,2:T(8,128)S(1)} %maximum_add_fusion.1), channel_id=1, source_target_pairs={{0,4},{4,8},{8,12},{12,16},{16,20},{20,24},{24,28},{28,32},{32,36}... | collective-permute-start | bytes 1572872 | tf_op jit(solution)/shard_map/ppermute | solution.py:23
  142.0 2.4 %copy-start.5 = (bf16[128,4,128]{2,0,1:T(8,128)(2,1)S(1)}, bf16[128,4,128]{2,0,1:T(8,128)(2,1)}, u32[]{:S(2)}) copy-start(bf16[128,4,128]{2,0,1:T(8,128)(2,1)} %copy-done.4) | copy-start | bytes 393220
  142.0 23.5 %collective-permute-start.9 = (f32[128,4,2,128]{3,0,1,2:T(8,128)S(1)}, f32[128,4,2,128]{3,0,1,2:T(8,128)S(1)}, u32[]{:S(2)}, u32[]{:S(2)}) collective-permute-start(f32[128,4,2,128]{3,0,1,2:T(8,128)S(1)} %maximum_add_fusion.2), channel_id=1, source_target_pairs={{0,1012},{4,1016},{8,1020},{12,0},{16,4},{20,8},{24,12},{28,16},{3... | collective-permute-start | bytes 1572872 | tf_op jit(solution)/shard_map/ppermute | solution.py:23
where the time goes:
time: 185 us; the launch traced here: 183 us
  waiting for transfers between devices  129 us (70%)
  starting transfers between devices  24.1 us (13%)
  blocking collectives  16.2 us (9%)
  local copies, waits for them, and re-layouts  5.26 us (3%)
  matrix products  4.94 us (3%)
  other arithmetic  2.62 us (1%)
    ppermute x4, waiting for transfers between devices, from_behind(): return lax.ppermute(value, axis, pairs)  86.4 us
    ppermute x6, waiting for transfers between devices, passed_along(): return lax.ppermute(x, axis, pairs)  42.2 us
    ppermute x6, starting transfers between devices, passed_along(): return lax.ppermute(x, axis, pairs)  16.3 us
    unnamed x1, blocking collectives  16.2 us
    ppermute x4, starting transfers between devices, from_behind(): return lax.ppermute(value, axis, pairs)  7.81 us
    unnamed x30, local copies, waits for them, and re-layouts  3.95 us
  transfers between devices with their start and end apart: 10, of which 10 were waited for; matrix products, arithmetic and copies ran while one was open for 4% of the time, Pallas kernels for 0%

commit v1 on v0

v1 whole, which is shorter than its diff:
```python
import jax
import jax.numpy as jnp
from jax import lax
from jax.experimental import pallas as pl
from jax.experimental.pallas import tpu as pltpu
from jax.sharding import PartitionSpec as P

SPAN = 4
HEADS = 4
LOWEST = -1e30
LOG2E = 1.4426950408889634
MESH = pl.DeviceIdType.MESH
NT = (((1,), (1,)), ((), ()))


def kernel(
    len_ref, qo_ref, kv_ref,
    dq_ref, dkv_ref,
    qo_all, kv_all, kt_all, e_all, dp_all, ds_all, m_all, t_all, w_all, g_out, g_in, dq_out,
    qo_send, qo_recv, kv_send, kv_recv, g_send, g_recv, dq_send, dq_recv,
):
    ctx = lax.axis_index("ctx")
    head = lax.axis_index("head")
    count = lax.axis_size("ctx")
    width = kv_ref.shape[1]
    depth = kv_ref.shape[2]
    rows = qo_ref.shape[2]
    factor = depth ** -0.5

    def ctx_at(shift):
        return lax.rem(ctx + (shift + count), count)

    def head_at(shift):
        return lax.rem(head + (shift + HEADS), HEADS)

    barrier = pltpu.get_barrier_semaphore()
    for s in range(1, SPAN):
        for sign in (1, -1):
            pl.semaphore_signal(
                barrier, inc=1, device_id={"ctx": ctx_at(sign * s), "head": head}, device_id_type=MESH
            )
    for k in range(1, HEADS):
        pl.semaphore_signal(
            barrier, inc=1, device_id={"ctx": ctx, "head": head_at(k)}, device_id_type=MESH
        )
    pl.semaphore_wait(barrier, 2 * (SPAN - 1) + HEADS - 1)

    kv_copies = []
    for s in range(1, SPAN):
        copy = pltpu.make_async_remote_copy(
            src_ref=kv_ref, dst_ref=kv_all.at[s - 1],
            send_sem=kv_send.at[s - 1], recv_sem=kv_recv.at[s - 1],
            device_id={"ctx": ctx_at(s), "head": head}, device_id_type=MESH,
        )
        copy.start()
        kv_copies.append(copy)
    qo_copies = []
    for k in range(1, HEADS):
        target = head_at(k)
        copy = pltpu.make_async_remote_copy(
            src_ref=qo_ref.at[target], dst_ref=qo_all.at[k - 1],
            send_sem=qo_send.at[k - 1], recv_sem=qo_recv.at[k - 1],
            device_id={"ctx": ctx, "head": target}, device_id_type=MESH,
        )
        copy.start()
        qo_copies.append(copy)

    lengths = len_ref[...]
    down = lax.broadcasted_iota(jnp.int32, (width, width), 0)
    across = lax.broadcasted_iota(jnp.int32, (width, width), 1)
    spread = jnp.broadcast_to(lengths, (width, width)).astype(jnp.float32)
    ends = jnp.sum(jnp.where(across <= down, spread, 0.0), axis=1, keepdims=True)
    own = jnp.sum(jnp.where(across == down, spread, 0.0), axis=1, keepdims=True)
    query_pos = ctx * width + across
    start = jnp.sum(
        jnp.where(ends <= query_pos.astype(jnp.float32), own, 0.0), axis=0, keepdims=True
    ).astype(jnp.int32)

    def qo(k):
        return qo_ref.at[head] if k == 0 else qo_all.at[k - 1]

    def kv(s):
        return kv_ref if s == 0 else kv_all.at[s - 1]

    scale = factor * LOG2E
    for s in range(SPAN):
        if s:
            kv_copies[s - 1].wait_recv()
        keys = kv(s)[0]
        values = kv(s)[1]
        kt_all[:, s * width:(s + 1) * width] = keys.T
        key_pos = (ctx - s) * width + down
        allowed = (key_pos >= start) & (key_pos <= query_pos)
        bias = jnp.where(allowed, 0.0, LOWEST)
        bias = jnp.concatenate([bias] * (rows // width), axis=1)
        for k in range(HEADS):
            if s == 0 and k:
                qo_copies[k - 1].wait_recv()
            cols = slice(k * rows, (k + 1) * rows)
            score = lax.dot_general(keys, qo(k)[0], NT, preferred_element_type=jnp.float32) + bias
            dprob = lax.dot_general(values, qo(k)[1], NT, preferred_element_type=jnp.float32)
            peak = jnp.max(score, axis=0, keepdims=True)
            expo = jnp.exp2((score - peak) * scale)
            m_all[s, :, cols] = peak
            t_all[s, :, cols] = jnp.sum(expo, axis=0, keepdims=True)
            w_all[s, :, cols] = jnp.sum(expo * dprob, axis=0, keepdims=True)
            e_all[s, :, cols] = expo
            dp_all[s, :, cols] = dprob

    peaks = [m_all[s] for s in range(SPAN)]
    peak = jnp.maximum(jnp.maximum(peaks[0], peaks[1]), jnp.maximum(peaks[2], peaks[3]))
    shares = [jnp.exp2((p - peak) * scale) for p in peaks]
    total = sum(t_all[s] * shares[s] for s in range(SPAN))
    inverse = 1.0 / total
    delta = sum(w_all[s] * shares[s] for s in range(SPAN)) * inverse
    shares = [share * inverse for share in shares]

    g_copies = []
    mine = None
    for s in (3, 2, 1, 0):
        keys_part = jnp.zeros((width, depth), jnp.float32)
        values_part = jnp.zeros((width, depth), jnp.float32)
        for k in range(HEADS):
            cols = slice(k * rows, (k + 1) * rows)
            prob = e_all[s, :, cols] * shares[s][:, cols]
            dscore = (prob * (dp_all[s, :, cols] - delta[:, cols])).astype(jnp.bfloat16)
            ds_all[s * width:(s + 1) * width, cols] = dscore
            keys_part += jnp.dot(dscore, qo(k)[0], preferred_element_type=jnp.float32)
            values_part += jnp.dot(
                prob.astype(jnp.bfloat16), qo(k)[1], preferred_element_type=jnp.float32
            )
        keys_part = keys_part * factor
        if s:
            g_out[s - 1, 0] = keys_part.astype(jnp.bfloat16)
            g_out[s - 1, 1] = values_part.astype(jnp.bfloat16)
            copy = pltpu.make_async_remote_copy(
                src_ref=g_out.at[s - 1], dst_ref=g_in.at[s - 1],
                send_sem=g_send.at[s - 1], recv_sem=g_recv.at[s - 1],
                device_id={"ctx": ctx_at(-s), "head": head}, device_id_type=MESH,
            )
            copy.start()
            g_copies.append(copy)
        else:
            mine = (keys_part, values_part)

    dq_copies = []
    for k in (1, 2, 3, 0):
        cols = slice(k * rows, (k + 1) * rows)
        dq = jnp.dot(kt_all[...], ds_all[:, cols], preferred_element_type=jnp.float32)
        dq = (dq.T * factor).astype(jnp.bfloat16)
        if k:
            dq_out[k - 1] = dq
            copy = pltpu.make_async_remote_copy(
                src_ref=dq_out.at[k - 1], dst_ref=dq_ref.at[head],
                send_sem=dq_send.at[k - 1], recv_sem=dq_recv.at[k - 1],
                device_id={"ctx": ctx, "head": head_at(-k)}, device_id_type=MESH,
            )
            copy.start()
            dq_copies.append(copy)
        else:
            dq_ref[head] = dq

    for copy in g_copies:
        copy.wait_recv()
    for i in range(2):
        acc = mine[i]
        for s in range(1, SPAN):
            acc = acc + g_in[s - 1, i].astype(jnp.float32)
        dkv_ref[i] = acc.astype(jnp.bfloat16)
    for k, copy in zip((1, 2, 3), dq_copies):
        pltpu.make_async_remote_copy(
            src_ref=dq_out.at[k - 1], dst_ref=dq_ref.at[head_at(k)],
            send_sem=dq_send.at[k - 1], recv_sem=dq_recv.at[k - 1],
            device_id={"ctx": ctx, "head": head_at(-k)}, device_id_type=MESH,
        ).wait_recv()
    for copy in kv_copies + qo_copies + g_copies + dq_copies:
        copy.wait_send()


def on_device(queries, keys, values, out_grad, lengths):
    width, group, heads, depth = queries.shape
    head = lax.axis_index("head")
    rows = group * width
    qo = jnp.stack([queries, out_grad]).transpose(3, 0, 2, 1, 4).reshape(heads, 2, rows, depth)
    kv = jnp.stack([
        lax.dynamic_index_in_dim(keys, head, 1, keepdims=False),
        lax.dynamic_index_in_dim(values, head, 1, keepdims=False),
    ])
    vmem = pl.BlockSpec(memory_space=pltpu.VMEM)
    bf16, f32 = jnp.bfloat16, jnp.float32
    total_q = HEADS * rows
    dma = pltpu.SemaphoreType.DMA((3,))
    dq, dkv = pl.pallas_call(
        kernel,
        out_shape=(
            jax.ShapeDtypeStruct((heads, rows, depth), bf16),
            jax.ShapeDtypeStruct((2, width, depth), bf16),
        ),
        in_specs=[vmem] * 3,
        out_specs=(vmem, vmem),
        scratch_shapes=[
            pltpu.VMEM((HEADS - 1, 2, rows, depth), bf16),
            pltpu.VMEM((SPAN - 1, 2, width, depth), bf16),
            pltpu.VMEM((depth, SPAN * width), bf16),
            pltpu.VMEM((SPAN, width, total_q), f32),
            pltpu.VMEM((SPAN, width, total_q), f32),
            pltpu.VMEM((SPAN * width, total_q), bf16),
            pltpu.VMEM((SPAN, 1, total_q), f32),
            pltpu.VMEM((SPAN, 1, total_q), f32),
            pltpu.VMEM((SPAN, 1, total_q), f32),
            pltpu.VMEM((SPAN - 1, 2, width, depth), bf16),
            pltpu.VMEM((SPAN - 1, 2, width, depth), bf16),
            pltpu.VMEM((HEADS - 1, rows, depth), bf16),
        ] + [dma] * 8,
        compiler_params=pltpu.CompilerParams(
            collective_id=0, has_side_effects=True, vmem_limit_bytes=32 * 2 ** 20
        ),
    )(lengths.reshape(1, -1), qo, kv)
    query_grad = dq.reshape(heads, group, width, depth).transpose(2, 1, 0, 3)
    return query_grad, dkv[0][:, None, :], dkv[1][:, None, :]


def solution(mesh):
    in_specs = (
        P("ctx", "head", None, None),
        P("ctx", None, None),
        P("ctx", None, None),
        P("ctx", "head", None, None),
        P(),
    )
    out_specs = (P("ctx", "head", None, None), P("ctx", "head", None), P("ctx", "head", None))
    return jax.shard_map(
        on_device, mesh=mesh, in_specs=in_specs, out_specs=out_specs, check_vma=False
    )
```

time: 185 us -> 50 us (0.27)
  the two profiles are of different devices: /device:TPU:6 before, /device:TPU:9 now
where the time goes in v1:
time: 50 us; the launch traced here: 49.8 us
  Pallas kernels  44.4 us (89%)
  local copies, waits for them, and re-layouts  3.27 us (7%)
  other arithmetic  1.43 us (3%)
  between operations  0.71 us (1%)
    pallas_call x1, Pallas kernels, on_device(): pl.pallas_call(kernel, out_shape=(jax.ShapeDtypeStruct((heads, rows, dept...  44.4 us
    unnamed x8, local copies, waits for them, and re-layouts  1.5 us
    transpose x1, other arithmetic, on_device(): jnp.stack([queries, out_grad]).transpose(3, 0, 2, 1, 4)  1.42 us

profile of v1, /device:TPU:9, one launch (start us, length us, event | category | flops | bytes accessed | tf_op | source)
XLA Modules:
  0.0 49.8 jit_solution(8152312902321400590)
XLA Ops:
  0.6 1.4 %maximum_bitcast_fusion = bf16[4,2,2,128,128]{4,0,2,3,1:T(4,128)(2,1)S(1)} fusion(bf16[1,128,2,4,128]{4,3,2,1,0:T(4,128)(2,1)} %bitcast.24, bf16[1,128,2,4,128]{4,3,2,1,0:T(4,128)(2,1)} %bitcast.25), kind=kLoop, calls=%fused_computation | loop fusion | flops 262144 | bytes 1048576 | tf_op jit(solution)/shard_map/transpose | solution.py:184
  2.1 0.0 copy-start.1
  2.1 0.0 copy-start.2
  2.1 0.1 copy.10
  2.2 0.8 %copy-done.1 = bf16[128,4,128]{2,1,0:T(4,128)(2,1)S(1)} copy-done((bf16[128,4,128]{2,1,0:T(4,128)(2,1)S(1)}, bf16[128,4,128]{2,1,0:T(4,128)(2,1)}, u32[]{:S(2)}) %copy-start.1) | copy-done | bytes 131096
  3.0 0.1 copy-done.2
  3.0 0.1 constant_dynamic-slice_fusion
  3.2 0.0 copy-start
  3.2 0.6 %copy-done = s32[128]{0:T(128)S(1)} copy-done((s32[128]{0:T(128)S(1)}, s32[128]{0:T(128)}, u32[]{:S(2)}) %copy-start) | copy-done | bytes 536
  3.9 44.4 %shard_map.76 = (bf16[4,256,128]{2,1,0:T(8,128)(2,1)S(1)}, bf16[2,128,128]{2,1,0:T(8,128)(2,1)S(1)}) custom-call(s32[1,128]{1,0:T(1,128)S(1)} %bitcast.22, bf16[4,2,256,128]{3,2,1,0:T(8,128)(2,1)S(1)} %bitcast.20, bf16[2,128,128]{2,1,0:T(8,128)(2,1)S(1)} %pad_maximum_fusion.kv_ref), custom_call_target="tpu_custom_call" | custom-call | tf_op jit(solution)/shard_map/pallas_call | solution.py:193
  48.3 0.9 %copy.19 = bf16[4,2,128,128]{3,0,1,2:T(4,128)(2,1)} copy(bf16[4,2,128,128]{3,2,1,0:T(8,128)(2,1)S(1)} %bitcast.21) | data formatting | bytes 524288 | tf_op jit(solution)/shard_map/reshape | solution.py:219
  49.2 0.6 %slice_bitcast_fusion = (bf16[128,1,128]{2,0,1:T(8,128)(2,1)}, bf16[128,1,128]{2,0,1:T(8,128)(2,1)}) fusion(bf16[2,128,128]{2,1,0:T(8,128)(2,1)S(1)} %get-tuple-element.6), kind=kLoop, calls=%fused_computation.5 | loop fusion | bytes 131072 | tf_op jit(solution)/shard_map/broadcast_in_dim;squeeze | solution.py:220
  (3 shorter events, 0.0 us)
Async XLA Ops:
  2.1 0.9 %copy-start.1 = (bf16[128,4,128]{2,1,0:T(4,128)(2,1)S(1)}, bf16[128,4,128]{2,1,0:T(4,128)(2,1)}, u32[]{:S(2)}) copy-start(bf16[128,4,128]{2,1,0:T(4,128)(2,1)} %param.7) | copy-start | bytes 393220
  2.1 1.0 %copy-start.2 = (bf16[128,4,128]{2,1,0:T(4,128)(2,1)S(1)}, bf16[128,4,128]{2,1,0:T(4,128)(2,1)}, u32[]{:S(2)}) copy-start(bf16[128,4,128]{2,1,0:T(4,128)(2,1)} %param.6) | copy-start | bytes 393220
  3.2 0.7 %copy-start = (s32[128]{0:T(128)S(1)}, s32[128]{0:T(128)}, u32[]{:S(2)}) copy-start(s32[128]{0:T(128)} %param.9) | copy-start | bytes 1540

commit v2 on v1

v2 whole, which is shorter than its diff:
```python
import jax
import jax.numpy as jnp
from jax import lax
from jax.experimental import pallas as pl
from jax.experimental.pallas import tpu as pltpu
from jax.sharding import PartitionSpec as P

SPAN = 4
HEADS = 4
LOWEST = -1e30
LOG2E = 1.4426950408889634
MESH = pl.DeviceIdType.MESH
NT = (((1,), (1,)), ((), ()))
BF16, F32, I32 = jnp.bfloat16, jnp.float32, jnp.int32


def one_hot(shape, column_of_row):
    row = lax.broadcasted_iota(I32, shape, 0)
    column = lax.broadcasted_iota(I32, shape, 1)
    return jnp.where(column == column_of_row(row), 1.0, 0.0).astype(BF16)


def kernel(
    len_hbm, q_hbm, k_hbm, v_hbm, o_hbm,
    dq_ref, dk_ref, dv_ref,
    len_in, q_in, k_in, v_in, o_in,
    qo_own, kv_own, qo_all, kv_all, kt_all, e_all, dp_all, ds_all, m_all, t_all, w_all,
    g_out, g_in, dq_out, dq_in,
    local, qo_send, qo_recv, kv_send, kv_recv, g_send, g_recv, dq_send, dq_recv,
):
    ctx = lax.axis_index("ctx")
    head = lax.axis_index("head")
    count = lax.axis_size("ctx")
    width, depth = kv_own.shape[1:]
    rows = qo_own.shape[2]
    group = rows // width
    slots = group * HEADS
    factor = depth ** -0.5

    def ctx_at(shift):
        return lax.rem(ctx + (shift + count), count)

    def head_at(shift):
        return lax.rem(head + (shift + HEADS), HEADS)

    def fetch(source, target, index):
        copy = pltpu.make_async_copy(source, target, local.at[index])
        copy.start()
        return copy

    def send(source, target, sems, index, ctx_shift=0, head_shift=0):
        copy = pltpu.make_async_remote_copy(
            src_ref=source, dst_ref=target, send_sem=sems[0].at[index], recv_sem=sems[1].at[index],
            device_id={"ctx": ctx_at(ctx_shift), "head": head_at(head_shift)}, device_id_type=MESH,
        )
        copy.start()
        return copy

    k_copy = fetch(k_hbm, k_in, 0)
    v_copy = fetch(v_hbm, v_in, 1)
    barrier = pltpu.get_barrier_semaphore()
    for s in range(1, SPAN):
        pl.semaphore_signal(
            barrier, inc=1, device_id={"ctx": ctx_at(-s), "head": head}, device_id_type=MESH
        )
    for k in range(1, HEADS):
        pl.semaphore_signal(
            barrier, inc=1, device_id={"ctx": ctx, "head": head_at(k)}, device_id_type=MESH
        )
    q_copy = fetch(q_hbm, q_in, 2)
    o_copy = fetch(o_hbm, o_in, 3)
    len_copy = fetch(len_hbm, len_in, 4)

    part = 2 * width
    tokens = part // HEADS
    pick = one_hot((tokens, part), lambda t: t * HEADS + head)
    k_copy.wait()
    v_copy.wait()
    for i in range(width // tokens):
        both = jnp.concatenate([k_in[i * part:(i + 1) * part], v_in[i * part:(i + 1) * part]], axis=1)
        both = jnp.dot(pick, both, preferred_element_type=F32).astype(BF16)
        kv_own[0, i * tokens:(i + 1) * tokens] = both[:, :depth]
        kv_own[1, i * tokens:(i + 1) * tokens] = both[:, depth:]

    pl.semaphore_wait(barrier, SPAN - 1 + HEADS - 1)
    kv_copies = [
        send(kv_own, kv_all.at[s - 1], (kv_send, kv_recv), s - 1, ctx_shift=s) for s in (3, 2, 1)
    ][::-1]

    tokens = part // slots
    order = one_hot((part, part), lambda r: lax.rem(r, tokens) * slots
                    + lax.rem(lax.div(r, tokens), group) * HEADS + lax.div(r, tokens * group))
    q_copy.wait()
    o_copy.wait()
    for i in range(width // tokens):
        both = jnp.concatenate([q_in[i * part:(i + 1) * part], o_in[i * part:(i + 1) * part]], axis=1)
        both = jnp.dot(order, both, preferred_element_type=F32).astype(BF16)
        for a in range(slots):
            g, j = divmod(a, group)
            here = slice(j * width + i * tokens, j * width + (i + 1) * tokens)
            qo_own[g, 0, here] = both[a * tokens:(a + 1) * tokens, :depth]
            qo_own[g, 1, here] = both[a * tokens:(a + 1) * tokens, depth:]
    qo_copies = [
        send(qo_own.at[head_at(k)], qo_all.at[k - 1], (qo_send, qo_recv), k - 1, head_shift=k)
        for k in range(1, HEADS)
    ]

    len_copy.wait()
    down = lax.broadcasted_iota(I32, (width, width), 0)
    across = lax.broadcasted_iota(I32, (width, width), 1)
    spread = jnp.broadcast_to(len_in[...], (width, width)).astype(F32)
    ends = jnp.sum(jnp.where(across <= down, spread, 0.0), axis=1, keepdims=True)
    own = jnp.sum(jnp.where(across == down, spread, 0.0), axis=1, keepdims=True)
    query_pos = ctx * width + across
    start = jnp.sum(
        jnp.where(ends <= query_pos.astype(F32), own, 0.0), axis=0, keepdims=True
    ).astype(I32)

    def qo(k):
        return qo_own.at[head] if k == 0 else qo_all.at[k - 1]

    def kv(s):
        return kv_own if s == 0 else kv_all.at[s - 1]

    scale = factor * LOG2E
    for s in range(SPAN):
        if s:
            kv_copies[s - 1].wait_recv()
        keys = kv(s)[0]
        values = kv(s)[1]
        kt_all[:, s * width:(s + 1) * width] = keys.T
        key_pos = (ctx - s) * width + down
        allowed = (key_pos >= start) & (key_pos <= query_pos)
        bias = jnp.where(allowed, 0.0, LOWEST)
        bias = jnp.concatenate([bias] * group, axis=1)
        for k in range(HEADS):
            if s == 0 and k:
                qo_copies[k - 1].wait_recv()
            cols = slice(k * rows, (k + 1) * rows)
            score = lax.dot_general(keys, qo(k)[0], NT, preferred_element_type=F32) + bias
            dprob = lax.dot_general(values, qo(k)[1], NT, preferred_element_type=F32)
            peak = jnp.max(score, axis=0, keepdims=True)
            expo = jnp.exp2((score - peak) * scale)
            m_all[s, :, cols] = peak
            t_all[s, :, cols] = jnp.sum(expo, axis=0, keepdims=True)
            w_all[s, :, cols] = jnp.sum(expo * dprob, axis=0, keepdims=True)
            e_all[s, :, cols] = expo
            dp_all[s, :, cols] = dprob

    peaks = [m_all[s] for s in range(SPAN)]
    peak = jnp.maximum(jnp.maximum(peaks[0], peaks[1]), jnp.maximum(peaks[2], peaks[3]))
    shares = [jnp.exp2((p - peak) * scale) for p in peaks]
    total = sum(t_all[s] * shares[s] for s in range(SPAN))
    inverse = 1.0 / total
    delta = sum(w_all[s] * shares[s] for s in range(SPAN)) * inverse
    shares = [share * inverse for share in shares]

    g_copies = []
    mine = None
    for s in (1, 2, 3, 0):
        keys_part = jnp.zeros((width, depth), F32)
        values_part = jnp.zeros((width, depth), F32)
        for k in range(HEADS):
            cols = slice(k * rows, (k + 1) * rows)
            prob = e_all[s, :, cols] * shares[s][:, cols]
            dscore = (prob * (dp_all[s, :, cols] - delta[:, cols])).astype(BF16)
            ds_all[s * width:(s + 1) * width, cols] = dscore
            keys_part += jnp.dot(dscore, qo(k)[0], preferred_element_type=F32)
            values_part += jnp.dot(prob.astype(BF16), qo(k)[1], preferred_element_type=F32)
        keys_part = keys_part * factor
        if s:
            g_out[s - 1, 0] = keys_part.astype(BF16)
            g_out[s - 1, 1] = values_part.astype(BF16)
            g_copies.append(send(g_out.at[s - 1], g_in.at[s - 1], (g_send, g_recv), s - 1, ctx_shift=-s))
        else:
            mine = (keys_part, values_part)

    dq_copies = []
    for k in (1, 2, 3, 0):
        cols = slice(k * rows, (k + 1) * rows)
        dq = jnp.dot(kt_all[...], ds_all[:, cols], preferred_element_type=F32)
        dq = (dq.T * factor).astype(BF16)
        if k:
            dq_out[k - 1] = dq
            dq_copies.append(
                send(dq_out.at[k - 1], dq_in.at[head], (dq_send, dq_recv), k - 1, head_shift=-k)
            )
        else:
            dq_in[head] = dq

    back = one_hot((part, part), lambda r: (lax.rem(r, HEADS) * group
                   + lax.rem(lax.div(r, HEADS), group)) * tokens + lax.div(r, slots))
    for k in range(1, HEADS):
        pltpu.make_async_remote_copy(
            src_ref=dq_out.at[k - 1], dst_ref=dq_in.at[head_at(k)],
            send_sem=dq_send.at[k - 1], recv_sem=dq_recv.at[k - 1],
            device_id={"ctx": ctx, "head": head_at(-k)}, device_id_type=MESH,
        ).wait_recv()
    for i in range(width // tokens):
        pieces = []
        for a in range(slots):
            g, j = divmod(a, group)
            pieces.append(dq_in[g, j * width + i * tokens:j * width + (i + 1) * tokens])
        dq_ref[i * part:(i + 1) * part] = jnp.dot(
            back, jnp.concatenate(pieces, axis=0), preferred_element_type=F32
        ).astype(BF16)

    for copy in g_copies:
        copy.wait_recv()
    for i, ref in enumerate((dk_ref, dv_ref)):
        acc = mine[i]
        for s in range(1, SPAN):
            acc = acc + g_in[s - 1, i].astype(F32)
        ref[...] = acc.astype(BF16)
    for copy in kv_copies + qo_copies + g_copies + dq_copies:
        copy.wait_send()


def on_device(queries, keys, values, out_grad, lengths):
    width, group, heads, depth = queries.shape
    rows = group * width
    total_q = heads * rows
    hbm = pl.BlockSpec(memory_space=pltpu.HBM)
    vmem = pl.BlockSpec(memory_space=pltpu.VMEM)
    dma = pltpu.SemaphoreType.DMA((3,))
    dq, dk, dv = pl.pallas_call(
        kernel,
        out_shape=(
            jax.ShapeDtypeStruct((total_q, depth), BF16),
            jax.ShapeDtypeStruct((width, depth), BF16),
            jax.ShapeDtypeStruct((width, depth), BF16),
        ),
        in_specs=[hbm] * 5,
        out_specs=(vmem, vmem, vmem),
        scratch_shapes=[
            pltpu.VMEM((1, lengths.shape[0]), I32),
            pltpu.VMEM((total_q, depth), BF16),
            pltpu.VMEM((heads * width, depth), BF16),
            pltpu.VMEM((heads * width, depth), BF16),
            pltpu.VMEM((total_q, depth), BF16),
            pltpu.VMEM((heads, 2, rows, depth), BF16),
            pltpu.VMEM((2, width, depth), BF16),
            pltpu.VMEM((HEADS - 1, 2, rows, depth), BF16),
            pltpu.VMEM((SPAN - 1, 2, width, depth), BF16),
            pltpu.VMEM((depth, SPAN * width), BF16),
            pltpu.VMEM((SPAN, width, total_q), F32),
            pltpu.VMEM((SPAN, width, total_q), F32),
            pltpu.VMEM((SPAN * width, total_q), BF16),
            pltpu.VMEM((SPAN, 1, total_q), F32),
            pltpu.VMEM((SPAN, 1, total_q), F32),
            pltpu.VMEM((SPAN, 1, total_q), F32),
            pltpu.VMEM((SPAN - 1, 2, width, depth), BF16),
            pltpu.VMEM((SPAN - 1, 2, width, depth), BF16),
            pltpu.VMEM((HEADS - 1, rows, depth), BF16),
            pltpu.VMEM((HEADS, rows, depth), BF16),
            pltpu.SemaphoreType.DMA((5,)),
        ] + [dma] * 8,
        compiler_params=pltpu.CompilerParams(
            collective_id=0, has_side_effects=True, vmem_limit_bytes=62 * 2 ** 20
        ),
    )(
        lengths.reshape(1, -1),
        queries.reshape(total_q, depth),
        keys.reshape(heads * width, depth),
        values.reshape(heads * width, depth),
        out_grad.reshape(total_q, depth),
    )
    return dq.reshape(queries.shape), dk[:, None, :], dv[:, None, :]


def solution(mesh):
    in_specs = (
        P("ctx", "head", None, None),
        P("ctx", None, None),
        P("ctx", None, None),
        P("ctx", "head", None, None),
        P(),
    )
    out_specs = (P("ctx", "head", None, None), P("ctx", "head", None), P("ctx", "head", None))
    return jax.shard_map(
        on_device, mesh=mesh, in_specs=in_specs, out_specs=out_specs, check_vma=False
    )
```

time: 50 us -> 49.1 us (0.982)
  the two profiles are of different devices: /device:TPU:9 before, /device:TPU:8 now
where the time goes in v2:
time: 49.1 us; the launch traced here: 48.8 us
  Pallas kernels  45 us (92%)
  local copies, waits for them, and re-layouts  3.14 us (6%)
  between operations  0.65 us (1%)
    pallas_call x1, Pallas kernels, on_device(): pl.pallas_call(kernel, out_shape=(jax.ShapeDtypeStruct((total_q, depth),...  45 us
    unnamed x7, local copies, waits for them, and re-layouts  3.14 us

profile of v2, /device:TPU:8, one launch (start us, length us, event | category | flops | bytes accessed | tf_op | source)
XLA Modules:
  0.0 48.8 jit_solution(14862029239154835041)
XLA Ops:
  0.6 45.0 %shard_map.76 = (bf16[1024,128]{1,0:T(8,128)(2,1)}, bf16[128,128]{1,0:T(8,128)(2,1)}, bf16[128,128]{1,0:T(8,128)(2,1)}) custom-call(s32[1,128]{1,0:T(1,128)} %bitcast.15, bf16[1024,128]{1,0:T(8,128)(2,1)} %bitcast.9, bf16[512,128]{1,0:T(8,128)(2,1)} %bitcast.11, bf16[512,128]{1,0:T(8,128)(2,1)} %bitcast.12, bf16[1024,128]{1,0:T(8,128)(2,1)} %bitcast.10), custom_call_target="tpu_custom_call" | custom-call | tf_op jit(solution)/shard_map/pallas_call | solution.py:226
  45.7 0.0 copy-start.1
  45.7 1.7 %copy.11 = bf16[128,2,4,128]{3,2,1,0:T(4,128)(2,1)} copy(bf16[128,2,4,128]{3,2,1,0:T(4,128)(2,1)} %bitcast.8) | data formatting | bytes 524288
  47.4 0.0 copy-done.1
  47.4 0.0 copy-start
  47.4 0.6 %copy.12 = bf16[128,1,128]{2,0,1:T(8,128)(2,1)} copy(bf16[128,1,128]{2,0,1:T(8,128)(2,1)S(1)} %bitcast.14) | data formatting | bytes 65536
  48.0 0.2 copy-done
  48.2 0.6 %copy.13 = bf16[128,1,128]{2,0,1:T(8,128)(2,1)} copy(bf16[128,1,128]{2,0,1:T(8,128)(2,1)S(1)} %bitcast.13) | data formatting | bytes 65536
Async XLA Ops:
  45.7 1.8 %copy-start.1 = (bf16[128,128]{1,0:T(8,128)(2,1)S(1)}, bf16[128,128]{1,0:T(8,128)(2,1)}, u32[]{:S(2)}) copy-start(bf16[128,128]{1,0:T(8,128)(2,1)} %get-tuple-element.7) | copy-start | bytes 98308
  47.4 0.8 %copy-start = (bf16[128,128]{1,0:T(8,128)(2,1)S(1)}, bf16[128,128]{1,0:T(8,128)(2,1)}, u32[]{:S(2)}) copy-start(bf16[128,128]{1,0:T(8,128)(2,1)} %get-tuple-element.8) | copy-start | bytes 98308

commit v3 on v2

--- a/solution.py
+++ b/solution.py
@@ -22,7 +22,7 @@
 
 def kernel(
     len_hbm, q_hbm, k_hbm, v_hbm, o_hbm,
-    dq_ref, dk_ref, dv_ref,
+    dq_ref, dkv_ref,
     len_in, q_in, k_in, v_in, o_in,
     qo_own, kv_own, qo_all, kv_all, kt_all, e_all, dp_all, ds_all, m_all, t_all, w_all,
     g_out, g_in, dq_out, dq_in,
@@ -48,21 +48,32 @@
         copy.start()
         return copy
 
-    def send(source, target, sems, index, ctx_shift=0, head_shift=0):
-        copy = pltpu.make_async_remote_copy(
+    def remote(source, target, sems, index, ctx_shift=0, head_shift=0):
+        return pltpu.make_async_remote_copy(
             src_ref=source, dst_ref=target, send_sem=sems[0].at[index], recv_sem=sems[1].at[index],
             device_id={"ctx": ctx_at(ctx_shift), "head": head_at(head_shift)}, device_id_type=MESH,
         )
+
+    def send(*args, **kwargs):
+        copy = remote(*args, **kwargs)
         copy.start()
         return copy
+
+    def later(s):
+        return pl.when(ctx + s < count)
+
+    def earlier(s):
+        return pl.when(ctx >= s)
 
     k_copy = fetch(k_hbm, k_in, 0)
     v_copy = fetch(v_hbm, v_in, 1)
     barrier = pltpu.get_barrier_semaphore()
     for s in range(1, SPAN):
-        pl.semaphore_signal(
-            barrier, inc=1, device_id={"ctx": ctx_at(-s), "head": head}, device_id_type=MESH
-        )
+        @earlier(s)
+        def _(s=s):
+            pl.semaphore_signal(
+                barrier, inc=1, device_id={"ctx": ctx_at(-s), "head": head}, device_id_type=MESH
+            )
     for k in range(1, HEADS):
         pl.semaphore_signal(
             barrier, inc=1, device_id={"ctx": ctx, "head": head_at(k)}, device_id_type=MESH
@@ -82,10 +93,29 @@
         kv_own[0, i * tokens:(i + 1) * tokens] = both[:, :depth]
         kv_own[1, i * tokens:(i + 1) * tokens] = both[:, depth:]
 
-    pl.semaphore_wait(barrier, SPAN - 1 + HEADS - 1)
+    for s in range(SPAN):
+        @pl.when(ctx + s < count if s == SPAN - 1 else ctx + s == count - 1)
+        def _(s=s):
+            pl.semaphore_wait(barrier, HEADS - 1 + s)
+
+    for s in range(1, SPAN):
+        @pl.when(ctx < s)
+        def _(s=s):
+            kv_all[s - 1] = jnp.zeros((2, width, depth), BF16)
+
+        @pl.when(ctx + s >= count)
+        def _(s=s):
+            g_in[s - 1] = jnp.zeros((2, width, depth), BF16)
+
     kv_copies = [
-        send(kv_own, kv_all.at[s - 1], (kv_send, kv_recv), s - 1, ctx_shift=s) for s in (3, 2, 1)
-    ][::-1]
+        remote(kv_own, kv_all.at[s - 1], (kv_send, kv_recv), s - 1, ctx_shift=s) for s in range(1, SPAN)
+    ]
+    g_copies = [
+        remote(g_out.at[s - 1], g_in.at[s - 1], (g_send, g_recv), s - 1, ctx_shift=-s)
+        for s in range(1, SPAN)
+    ]
+    for s in (1, 2, 3):
+        later(s)(kv_copies[s - 1].start)
 
     tokens = part // slots
     order = one_hot((part, part), lambda r: lax.rem(r, tokens) * slots
@@ -116,6 +146,7 @@
         jnp.where(ends <= query_pos.astype(F32), own, 0.0), axis=0, keepdims=True
     ).astype(I32)
 
+
     def qo(k):
         return qo_own.at[head] if k == 0 else qo_all.at[k - 1]
 
@@ -125,7 +156,7 @@
     scale = factor * LOG2E
     for s in range(SPAN):
         if s:
-            kv_copies[s - 1].wait_recv()
+            earlier(s)(kv_copies[s - 1].wait_recv)
         keys = kv(s)[0]
         values = kv(s)[1]
         kt_all[:, s * width:(s + 1) * width] = keys.T
@@ -155,7 +186,6 @@
     delta = sum(w_all[s] * shares[s] for s in range(SPAN)) * inverse
     shares = [share * inverse for share in shares]
 
-    g_copies = []
     mine = None
     for s in (1, 2, 3, 0):
         keys_part = jnp.zeros((width, depth), F32)
@@ -171,7 +201,7 @@
         if s:
             g_out[s - 1, 0] = keys_part.astype(BF16)
             g_out[s - 1, 1] = values_part.astype(BF16)
-            g_copies.append(send(g_out.at[s - 1], g_in.at[s - 1], (g_send, g_recv), s - 1, ctx_shift=-s))
+            earlier(s)(g_copies[s - 1].start)
         else:
             mine = (keys_part, values_part)
 
@@ -187,6 +217,7 @@
             )
         else:
             dq_in[head] = dq
+
 
     back = one_hot((part, part), lambda r: (lax.rem(r, HEADS) * group
                    + lax.rem(lax.div(r, HEADS), group)) * tokens + lax.div(r, slots))
@@ -205,14 +236,17 @@
             back, jnp.concatenate(pieces, axis=0), preferred_element_type=F32
         ).astype(BF16)
 
-    for copy in g_copies:
-        copy.wait_recv()
-    for i, ref in enumerate((dk_ref, dv_ref)):
+    for s in range(1, SPAN):
+        later(s)(g_copies[s - 1].wait_recv)
+    for i in range(2):
         acc = mine[i]
         for s in range(1, SPAN):
             acc = acc + g_in[s - 1, i].astype(F32)
-        ref[...] = acc.astype(BF16)
-    for copy in kv_copies + qo_copies + g_copies + dq_copies:
+        dkv_ref[i] = acc.astype(BF16)
+    for s in range(1, SPAN):
+        later(s)(kv_copies[s - 1].wait_send)
+        earlier(s)(g_copies[s - 1].wait_send)
+    for copy in qo_copies + dq_copies:
         copy.wait_send()
 
 
@@ -223,15 +257,14 @@
     hbm = pl.BlockSpec(memory_space=pltpu.HBM)
     vmem = pl.BlockSpec(memory_space=pltpu.VMEM)
     dma = pltpu.SemaphoreType.DMA((3,))
-    dq, dk, dv = pl.pallas_call(
+    dq, dkv = pl.pallas_call(
         kernel,
         out_shape=(
-            jax.ShapeDtypeStruct((total_q, depth), BF16),
-            jax.ShapeDtypeStruct((width, depth), BF16),
-            jax.ShapeDtypeStruct((width, depth), BF16),
+            pltpu.VMEM((total_q, depth), BF16),
+            pltpu.VMEM((2, width, depth), BF16),
         ),
         in_specs=[hbm] * 5,
-        out_specs=(vmem, vmem, vmem),
+        out_specs=(vmem, vmem),
         scratch_shapes=[
             pltpu.VMEM((1, lengths.shape[0]), I32),
             pltpu.VMEM((total_q, depth), BF16),
@@ -265,7 +298,7 @@
         values.reshape(heads * width, depth),
         out_grad.reshape(total_q, depth),
     )
-    return dq.reshape(queries.shape), dk[:, None, :], dv[:, None, :]
+    return dq.reshape(queries.shape), dkv[0][:, None, :], dkv[1][:, None, :]
 
 
 def solution(mesh):

time: 49.1 us -> 41.2 us (0.84)
  the two profiles are of different devices: /device:TPU:8 before, /device:TPU:6 now
where the time goes in v3:
time: 41.2 us; the launch traced here: 41.1 us
  Pallas kernels  39.1 us (95%)
  local copies, waits for them, and re-layouts  1.33 us (3%)
  between operations  0.64 us (2%)
    pallas_call x1, Pallas kernels, on_device(): pl.pallas_call(kernel, out_shape=(pltpu.VMEM((total_q, depth), BF16), plt...  39.1 us

profile of v3, /device:TPU:6, one launch (start us, length us, event | category | flops | bytes accessed | tf_op | source)
XLA Modules:
  0.0 41.1 jit_solution(3267596822770259266)
XLA Ops:
  0.6 39.1 %shard_map.76 = (bf16[1024,128]{1,0:T(8,128)(2,1)S(1)}, bf16[2,128,128]{2,1,0:T(8,128)(2,1)S(1)}) custom-call(s32[1,128]{1,0:T(1,128)} %bitcast.15, bf16[1024,128]{1,0:T(8,128)(2,1)} %bitcast.11, bf16[512,128]{1,0:T(8,128)(2,1)} %bitcast.13, bf16[512,128]{1,0:T(8,128)(2,1)} %bitcast.14, bf16[1024,128]{1,0:T(8,128)(2,1)} %bitcast.12), custom_call_target="tpu_custom_call" | custom-call | tf_op jit(solution)/shard_map/pallas_call | solution.py:260
  39.7 0.7 %copy.9 = bf16[128,2,4,128]{3,2,1,0:T(4,128)(2,1)} copy(bf16[128,2,4,128]{3,2,1,0:T(4,128)(2,1)S(1)} %bitcast.10) | data formatting | bytes 524288
  40.4 0.6 %slice_bitcast_fusion = (bf16[128,1,128]{2,0,1:T(8,128)(2,1)}, bf16[128,1,128]{2,0,1:T(8,128)(2,1)}) fusion(bf16[2,128,128]{2,1,0:T(8,128)(2,1)S(1)} %get-tuple-element.6), kind=kLoop, calls=%fused_computation | loop fusion | bytes 131072 | tf_op jit(solution)/shard_map/broadcast_in_dim;squeeze | solution.py:301

commit v4 on v3

--- a/solution.py
+++ b/solution.py
@@ -6,6 +6,7 @@
 from jax.sharding import PartitionSpec as P
 
 SPAN = 4
+ROW = 16
 HEADS = 4
 LOWEST = -1e30
 LOG2E = 1.4426950408889634
@@ -31,6 +32,7 @@
     ctx = lax.axis_index("ctx")
     head = lax.axis_index("head")
     count = lax.axis_size("ctx")
+    place = lax.rem(ctx, ROW)
     width, depth = kv_own.shape[1:]
     rows = qo_own.shape[2]
     group = rows // width
@@ -201,7 +203,7 @@
         if s:
             g_out[s - 1, 0] = keys_part.astype(BF16)
             g_out[s - 1, 1] = values_part.astype(BF16)
-            earlier(s)(g_copies[s - 1].start)
+            pl.when((ctx >= s) & ((place == 0) | (place >= s)))(g_copies[s - 1].start)
         else:
             mine = (keys_part, values_part)
 
@@ -219,6 +221,9 @@
             dq_in[head] = dq
 
 
+    for s in range(2, SPAN):
+        pl.when((place == 1) & (ctx >= s))(g_copies[s - 1].start)
+
     back = one_hot((part, part), lambda r: (lax.rem(r, HEADS) * group
                    + lax.rem(lax.div(r, HEADS), group)) * tokens + lax.div(r, slots))
     for k in range(1, HEADS):
@@ -227,6 +232,7 @@
             send_sem=dq_send.at[k - 1], recv_sem=dq_recv.at[k - 1],
             device_id={"ctx": ctx, "head": head_at(-k)}, device_id_type=MESH,
         ).wait_recv()
+    pl.when((place == 2) & (ctx >= 3))(g_copies[2].start)
     for i in range(width // tokens):
         pieces = []
         for a in range(slots):
@@ -248,6 +254,15 @@
         earlier(s)(g_copies[s - 1].wait_send)
     for copy in qo_copies + dq_copies:
         copy.wait_send()
+
+
+def store(dq_ref, dkv_ref, dq_hbm, dk_hbm, dv_hbm, sems):
+    pairs = ((dq_ref, dq_hbm), (dkv_ref.at[0], dk_hbm), (dkv_ref.at[1], dv_hbm))
+    copies = [pltpu.make_async_copy(a, b, sems.at[i]) for i, (a, b) in enumerate(pairs)]
+    for copy in copies:
+        copy.start()
+    for copy in copies:
+        copy.wait()
 
 
 def on_device(queries, keys, values, out_grad, lengths):
@@ -298,7 +313,20 @@
         values.reshape(heads * width, depth),
         out_grad.reshape(total_q, depth),
     )
-    return dq.reshape(queries.shape), dkv[0][:, None, :], dkv[1][:, None, :]
+    vin = pl.BlockSpec(memory_space=pltpu.VMEM)
+    dq, dk, dv = pl.pallas_call(
+        store,
+        out_shape=(
+            jax.ShapeDtypeStruct((total_q, depth), BF16),
+            jax.ShapeDtypeStruct((width, depth), BF16),
+            jax.ShapeDtypeStruct((width, depth), BF16),
+        ),
+        in_specs=[pl.BlockSpec(memory_space=pl.ANY)] * 2,
+        out_specs=(hbm, hbm, hbm),
+        scratch_shapes=[pltpu.SemaphoreType.DMA((3,))],
+        compiler_params=pltpu.CompilerParams(vmem_limit_bytes=4 * 2 ** 20),
+    )(dq, dkv)
+    return dq.reshape(queries.shape), dk[:, None, :], dv[:, None, :]
 
 
 def solution(mesh):

time: 41.2 us -> 39.5 us (0.959)
  local copies, waits for them, and re-layouts: 1.33 us -> 0 us
  Pallas kernels: 39.1 us -> 38.4 us
    pallas_call x1, Pallas kernels: 39.1 us -> 37.6 us  [on_device(): pl.pallas_call(kernel, out_shape=(pltpu.VMEM((total_q, depth), BF16), plt...]
    pallas_call x0 -> x1, Pallas kernels: none -> 0.74 us  [on_device(): pl.pallas_call(store, out_shape=(jax.ShapeDtypeStruct((total_q, depth), B...]
    unnamed x1 -> x0, local copies, waits for them, and re-layouts: 0.71 us -> none
    another operation x1 -> x0, local copies, waits for them, and re-layouts: 0.63 us -> none  [on_device(): return (dq.reshape(queries.shape), dkv[0][:, None, :], dkv[1][:, None, :])]
where the time goes in v4:
time: 39.5 us; the launch traced here: 39 us
  Pallas kernels  38.4 us (97%)
  between operations  0.64 us (2%)
    pallas_call x1, Pallas kernels, on_device(): pl.pallas_call(kernel, out_shape=(pltpu.VMEM((total_q, depth), BF16), plt...  37.6 us

profile of v4, /device:TPU:6, one launch (start us, length us, event | category | flops | bytes accessed | tf_op | source)
XLA Modules:
  0.0 39.0 jit_solution(15276460071489577693)
XLA Ops:
  0.6 37.6 %shard_map.76 = (bf16[1024,128]{1,0:T(8,128)(2,1)S(1)}, bf16[2,128,128]{2,1,0:T(8,128)(2,1)S(1)}) custom-call(s32[1,128]{1,0:T(1,128)} %bitcast.12, bf16[1024,128]{1,0:T(8,128)(2,1)} %bitcast.8, bf16[512,128]{1,0:T(8,128)(2,1)} %bitcast.10, bf16[512,128]{1,0:T(8,128)(2,1)} %bitcast.11, bf16[1024,128]{1,0:T(8,128)(2,1)} %bitcast.9), custom_call_target="tpu_custom_call" | custom-call | tf_op jit(solution)/shard_map/pallas_call | solution.py:275
  38.3 0.7 %shard_map.77 = (bf16[1024,128]{1,0:T(8,128)(2,1)}, bf16[128,128]{1,0:T(8,128)(2,1)}, bf16[128,128]{1,0:T(8,128)(2,1)}) custom-call(bf16[1024,128]{1,0:T(8,128)(2,1)S(1)} %get-tuple-element.8.dq_ref, bf16[2,128,128]{2,1,0:T(8,128)(2,1)S(1)} %get-tuple-element.9.dkv_ref), custom_call_target="tpu_custom_call" | custom-call | tf_op jit(solution)/shard_map/pallas_call | solution.py:317

commit v5 on v4

--- a/solution.py
+++ b/solution.py
@@ -27,7 +27,7 @@
     len_in, q_in, k_in, v_in, o_in,
     qo_own, kv_own, qo_all, kv_all, kt_all, e_all, dp_all, ds_all, m_all, t_all, w_all,
     g_out, g_in, dq_out, dq_in,
-    local, qo_send, qo_recv, kv_send, kv_recv, g_send, g_recv, dq_send, dq_recv,
+    local, qo_send, qo_recv, kv_send, relay_send, kv_recv, g_send, g_recv, dq_send, dq_recv,
 ):
     ctx = lax.axis_index("ctx")
     head = lax.axis_index("head")
@@ -51,8 +51,9 @@
         return copy
 
     def remote(source, target, sems, index, ctx_shift=0, head_shift=0):
+        sender, receiver = index if isinstance(index, tuple) else (index, index)
         return pltpu.make_async_remote_copy(
-            src_ref=source, dst_ref=target, send_sem=sems[0].at[index], recv_sem=sems[1].at[index],
+            src_ref=source, dst_ref=target, send_sem=sems[0].at[sender], recv_sem=sems[1].at[receiver],
             device_id={"ctx": ctx_at(ctx_shift), "head": head_at(head_shift)}, device_id_type=MESH,
         )
 
@@ -66,6 +67,12 @@
 
     def earlier(s):
         return pl.when(ctx >= s)
+
+    def direct(s):
+        return (ctx + s < count) & ((place + s != ROW) | (s != 2))
+
+    def relay():
+        return pl.when((place == 1) & (ctx > ROW))
 
     k_copy = fetch(k_hbm, k_in, 0)
     v_copy = fetch(v_hbm, v_in, 1)
@@ -116,8 +123,13 @@
         remote(g_out.at[s - 1], g_in.at[s - 1], (g_send, g_recv), s - 1, ctx_shift=-s)
         for s in range(1, SPAN)
     ]
+    passed_on = remote(kv_all.at[2], kv_all.at[1], (relay_send, kv_recv), (0, 1), ctx_shift=-1)
+    for s in (3, 1):
+        pl.when(direct(s) & (place == ROW - 2))(kv_copies[s - 1].start)
     for s in (1, 2, 3):
-        later(s)(kv_copies[s - 1].start)
+        pl.when(direct(s) & (place == ROW - 3))(kv_copies[s - 1].start)
+    for s in (1, 2, 3):
+        pl.when(direct(s) & ((place < ROW - 3) | (place == ROW - 1)))(kv_copies[s - 1].start)
 
     tokens = part // slots
     order = one_hot((part, part), lambda r: lax.rem(r, tokens) * slots
@@ -156,9 +168,11 @@
         return kv_own if s == 0 else kv_all.at[s - 1]
 
     scale = factor * LOG2E
-    for s in range(SPAN):
+    for s in (0, 1, 3, 2):
         if s:
             earlier(s)(kv_copies[s - 1].wait_recv)
+            if s == 3:
+                relay()(passed_on.start)
         keys = kv(s)[0]
         values = kv(s)[1]
         kt_all[:, s * width:(s + 1) * width] = keys.T
@@ -208,7 +222,7 @@
             mine = (keys_part, values_part)
 
     dq_copies = []
-    for k in (1, 2, 3, 0):
+    for k in (2, 1, 3, 0):
         cols = slice(k * rows, (k + 1) * rows)
         dq = jnp.dot(kt_all[...], ds_all[:, cols], preferred_element_type=F32)
         dq = (dq.T * factor).astype(BF16)
@@ -250,8 +264,9 @@
             acc = acc + g_in[s - 1, i].astype(F32)
         dkv_ref[i] = acc.astype(BF16)
     for s in range(1, SPAN):
-        later(s)(kv_copies[s - 1].wait_send)
+        pl.when(direct(s))(kv_copies[s - 1].wait_send)
         earlier(s)(g_copies[s - 1].wait_send)
+    relay()(passed_on.wait_send)
     for copy in qo_copies + dq_copies:
         copy.wait_send()
 
@@ -302,7 +317,7 @@
             pltpu.VMEM((HEADS - 1, rows, depth), BF16),
             pltpu.VMEM((HEADS, rows, depth), BF16),
             pltpu.SemaphoreType.DMA((5,)),
-        ] + [dma] * 8,
+        ] + [dma] * 9,
         compiler_params=pltpu.CompilerParams(
             collective_id=0, has_side_effects=True, vmem_limit_bytes=62 * 2 ** 20
         ),

time: 39.5 us -> 39.3 us (level)
  no operation moved by 1% of the time
where the time goes in v5:
time: 39.3 us; the launch traced here: 38.7 us
  Pallas kernels  38.1 us (97%)
  between operations  0.64 us (2%)
    pallas_call x1, Pallas kernels, on_device(): pl.pallas_call(kernel, out_shape=(pltpu.VMEM((total_q, depth), BF16), plt...  37.3 us

profile of v5, /device:TPU:6, one launch (start us, length us, event | category | flops | bytes accessed | tf_op | source)
XLA Modules:
  0.0 38.7 jit_solution(8908092060757878000)
XLA Ops:
  0.6 37.3 %shard_map.76 = (bf16[1024,128]{1,0:T(8,128)(2,1)S(1)}, bf16[2,128,128]{2,1,0:T(8,128)(2,1)S(1)}) custom-call(s32[1,128]{1,0:T(1,128)} %bitcast.12, bf16[1024,128]{1,0:T(8,128)(2,1)} %bitcast.8, bf16[512,128]{1,0:T(8,128)(2,1)} %bitcast.10, bf16[512,128]{1,0:T(8,128)(2,1)} %bitcast.11, bf16[1024,128]{1,0:T(8,128)(2,1)} %bitcast.9), custom_call_target="tpu_custom_call" | custom-call | tf_op jit(solution)/shard_map/pallas_call | solution.py:290
  38.0 0.7 %shard_map.77 = (bf16[1024,128]{1,0:T(8,128)(2,1)}, bf16[128,128]{1,0:T(8,128)(2,1)}, bf16[128,128]{1,0:T(8,128)(2,1)}) custom-call(bf16[1024,128]{1,0:T(8,128)(2,1)S(1)} %get-tuple-element.8.dq_ref, bf16[2,128,128]{2,1,0:T(8,128)(2,1)S(1)} %get-tuple-element.9.dkv_ref), custom_call_target="tpu_custom_call" | custom-call | tf_op jit(solution)/shard_map/pallas_call | solution.py:332

commit v6 on v5

--- a/solution.py
+++ b/solution.py
@@ -235,8 +235,7 @@
             dq_in[head] = dq
 
 
-    for s in range(2, SPAN):
-        pl.when((place == 1) & (ctx >= s))(g_copies[s - 1].start)
+    pl.when((place == 1) & (ctx >= 2))(g_copies[1].start)
 
     back = one_hot((part, part), lambda r: (lax.rem(r, HEADS) * group
                    + lax.rem(lax.div(r, HEADS), group)) * tokens + lax.div(r, slots))
@@ -246,7 +245,7 @@
             send_sem=dq_send.at[k - 1], recv_sem=dq_recv.at[k - 1],
             device_id={"ctx": ctx, "head": head_at(-k)}, device_id_type=MESH,
         ).wait_recv()
-    pl.when((place == 2) & (ctx >= 3))(g_copies[2].start)
+    pl.when(((place == 1) | (place == 2)) & (ctx >= 3))(g_copies[2].start)
     for i in range(width // tokens):
         pieces = []
         for a in range(slots):

time: 39.3 us -> 39.3 us (level)
  no operation moved by 1% of the time
where the time goes in v6:
time: 39.3 us; the launch traced here: 38.6 us
  Pallas kernels  38 us (97%)
  between operations  0.64 us (2%)
    pallas_call x1, Pallas kernels, on_device(): pl.pallas_call(kernel, out_shape=(pltpu.VMEM((total_q, depth), BF16), plt...  37.2 us

profile of v6, /device:TPU:6, one launch (start us, length us, event | category | flops | bytes accessed | tf_op | source)
XLA Modules:
  0.0 38.6 jit_solution(13134544032815946570)
XLA Ops:
  0.6 37.2 %shard_map.76 = (bf16[1024,128]{1,0:T(8,128)(2,1)S(1)}, bf16[2,128,128]{2,1,0:T(8,128)(2,1)S(1)}) custom-call(s32[1,128]{1,0:T(1,128)} %bitcast.12, bf16[1024,128]{1,0:T(8,128)(2,1)} %bitcast.8, bf16[512,128]{1,0:T(8,128)(2,1)} %bitcast.10, bf16[512,128]{1,0:T(8,128)(2,1)} %bitcast.11, bf16[1024,128]{1,0:T(8,128)(2,1)} %bitcast.9), custom_call_target="tpu_custom_call" | custom-call | tf_op jit(solution)/shard_map/pallas_call | solution.py:289
  37.9 0.7 %shard_map.77 = (bf16[1024,128]{1,0:T(8,128)(2,1)}, bf16[128,128]{1,0:T(8,128)(2,1)}, bf16[128,128]{1,0:T(8,128)(2,1)}) custom-call(bf16[1024,128]{1,0:T(8,128)(2,1)S(1)} %get-tuple-element.8.dq_ref, bf16[2,128,128]{2,1,0:T(8,128)(2,1)S(1)} %get-tuple-element.9.dkv_ref), custom_call_target="tpu_custom_call" | custom-call | tf_op jit(solution)/shard_map/pallas_call | solution.py:331
